TPU v7x, 256 devices: a whole 4x4x8 slice. The times are simulated.
256 devices in a mesh: dp: 32 (over y_hi, z, core), fsdp: 8 (over y_lo, x).
Axes of the slice: x: 4, y: 4 (y_hi: 2, y_lo: 2; y = y_hi * 2 + y_lo), z: 8, core: 2. Of those that a mesh axis runs over, the one named last changes fastest.
Arguments:
- hidden_act: bfloat16 [65536, 5120], P(('dp', 'fsdp')), may hold values from -6 to 6
- resid: bfloat16 [65536, 1280], P(('dp', 'fsdp')), may hold values from -6 to 6
- w_down: bfloat16 [5120, 1280], P('fsdp'), may hold values from -0.078125 to 0.078125
- norm_gain: float32 [1280], replicated, may hold values from 0.25 to 1.75
- w_proj: bfloat16 [1280, 1024], replicated, may hold values from -0.15625 to 0.15625
- optical: bfloat16 [1024, 1024], P(('dp', 'fsdp')), may hold values from -6 to 6
Outputs:
- d_hidden: bfloat16 [65536, 5120], P(('dp', 'fsdp'))
- d_resid: bfloat16 [65536, 1280], P(('dp', 'fsdp'))
- d_weight: float32 [5120, 1280], P('fsdp', 'dp')
All inputs are finite; a program needn't handle non-finite values.
Results may differ from a plain program's by a relative error of at most 0.04.
Values may be sent and summed in bfloat16 or wider, within the bound.
No kernel may reach another device: no remote copies, remote signals or barrier semaphores. Data moves between devices by JAX's collectives and lax.ppermute only.
A program may use at most 128 MiB of HBM per device.

v0:
```python
import jax
import jax.numpy as jnp
from jax import lax
from jax.sharding import PartitionSpec as P

PATCHES = 64


epsilon = 1e-06
logit_scale = 100.0


def body(hidden_act, resid, w_down, norm_gain, w_proj, optical):
    tok_rows = hidden_act.shape[0]
    images = tok_rows // PATCHES
    width = resid.shape[1]
    gathered = lax.all_gather(w_down, "fsdp", axis=0, tiled=True)
    branch = jnp.dot(hidden_act, gathered, preferred_element_type=jnp.float32)
    summed = resid.astype(jnp.float32) + branch
    center = jnp.mean(summed, axis=1, keepdims=True)
    spread = jnp.mean((summed - center) ** 2, axis=1, keepdims=True)
    inv_std = lax.rsqrt(spread + epsilon)
    normed = (summed - center) * inv_std
    scaled = normed * norm_gain
    pooled = scaled.reshape(images, PATCHES, width).mean(axis=1).astype(jnp.bfloat16)
    embed = jnp.dot(pooled, w_proj, preferred_element_type=jnp.float32)
    inv_len = lax.rsqrt(jnp.sum(embed * embed, axis=1, keepdims=True) + epsilon)
    sar_unit = embed * inv_len
    sar_half = sar_unit.astype(jnp.bfloat16)
    opt_full = optical.astype(jnp.float32)
    opt_unit = (
        opt_full * lax.rsqrt(jnp.sum(opt_full * opt_full, axis=1, keepdims=True) + epsilon)
    ).astype(jnp.bfloat16)
    every_opt = lax.all_gather(opt_unit, ("dp", "fsdp"), axis=0, tiled=True)
    contract = (((1,), (1,)), ((), ()))
    scores = logit_scale * lax.dot_general(
        sar_half, every_opt, contract, preferred_element_type=jnp.float32
    )
    powers = jnp.exp(scores)
    row_prob = powers / jnp.sum(powers, axis=1, keepdims=True)
    totals = lax.psum(jnp.sum(powers, axis=0), ("dp", "fsdp"))
    col_prob = powers / totals[None, :]
    first_pair = lax.axis_index(("dp", "fsdp")) * images
    positive = (
        lax.broadcasted_iota(jnp.int32, scores.shape, 1)
        == first_pair + lax.broadcasted_iota(jnp.int32, scores.shape, 0)
    ).astype(jnp.float32)
    weights = (row_prob + col_prob - 2.0 * positive).astype(jnp.bfloat16)
    grad_unit = 0.5 * logit_scale * jnp.dot(weights, every_opt, preferred_element_type=jnp.float32)
    grad_embed = inv_len * (
        grad_unit - sar_unit * jnp.sum(sar_unit * grad_unit, axis=1, keepdims=True)
    )
    grad_pooled = lax.dot_general(
        grad_embed.astype(jnp.bfloat16), w_proj, contract, preferred_element_type=jnp.float32
    )
    grad_tokens = jnp.broadcast_to(
        (grad_pooled / PATCHES)[:, None, :], (images, PATCHES, width)
    ).reshape(tok_rows, width)
    grad_normed = grad_tokens * norm_gain
    grad_sum = inv_std * (
        grad_normed
        - jnp.mean(grad_normed, axis=1, keepdims=True)
        - normed * jnp.mean(grad_normed * normed, axis=1, keepdims=True)
    )
    d_resid = grad_sum.astype(jnp.bfloat16)
    d_hidden = lax.dot_general(d_resid, gathered, contract, preferred_element_type=jnp.float32)
    d_hidden = d_hidden.astype(jnp.bfloat16)
    token_contract = (((0,), (0,)), ((), ()))
    term = lax.dot_general(hidden_act, d_resid, token_contract, preferred_element_type=jnp.float32)
    group_sum = lax.psum_scatter(
        term.astype(jnp.bfloat16).astype(jnp.float32).astype(jnp.bfloat16),
        "fsdp",
        scatter_dimension=0,
        tiled=True,
    )
    d_weight = lax.psum_scatter(group_sum, "dp", scatter_dimension=1, tiled=True).astype(
        jnp.float32
    )
    return (d_hidden, d_resid, d_weight)


def solution(mesh):
    in_specs = (
        P(("dp", "fsdp"), None),
        P(("dp", "fsdp"), None),
        P("fsdp", None),
        P(),
        P(),
        P(("dp", "fsdp"), None),
    )
    out_specs = (P(("dp", "fsdp"), None), P(("dp", "fsdp"), None), P("fsdp", "dp"))
    return jax.shard_map(body, mesh=mesh, in_specs=in_specs, out_specs=out_specs, check_vma=False)
```

profile of v0, /device:TPU:2, one launch (start us, length us, event | category | flops | bytes accessed | tf_op | source)
XLA Modules:
  0.0 1233.1 jit_solution(7799979125523033828)
XLA Ops:
  7.2 0.0 copy-start
  7.2 0.0 all-gather.6.cloned.1.call-start
  7.2 1.0 fusion.10
  8.2 1.4 fusion.16
  9.6 0.0 all-gather.6.cloned.1.call-update
  9.6 0.0 all-gather.4.cloned.1.call-start
  9.6 0.7 all-gather.4.cloned.1.call-update
  10.4 0.0 reduce-scatter.7.cloned.1.call-start
  10.4 0.0 copy-start.7
  10.4 695.2 %all-gather.6.cloned.1.call-done = bf16[256,4,1024]{2,1,0:T(4,128)(2,1)} async-done(((bf16[1,4,1024]{2,1,0:T(4,128)(2,1)}), bf16[256,4,1024]{2,1,0:T(4,128)(2,1)}) %all-gather.6.cloned.1.call-update) | async-done | bytes 2097168 | tf_op jit(solution)/shard_map/all_gather | solution.py:34
  705.7 3.9 reshape.62
  709.6 136.0 %all-gather.4.cloned.1.call-done = bf16[5120,1280]{1,0:T(8,128)(2,1)} async-done(((bf16[640,1280]{1,0:T(8,128)(2,1)}), bf16[5120,1280]{1,0:T(8,128)(2,1)}) %all-gather.4.cloned.1.call-update) | async-done | bytes 13107216 | tf_op jit(solution)/shard_map/all_gather | solution.py:17
  845.6 0.0 copy-done
  845.7 0.0 copy-done.7
  845.7 7.6 fusion.29
  853.2 0.0 copy-start.1
  853.2 0.0 copy-start.6
  853.2 0.0 copy-start.4
  853.3 0.3 multiply_reduce_fusion.1
  853.5 0.4 copy-done.6
  853.9 0.3 bitcast_reduce_fusion
  854.3 0.0 copy-done.1
  854.3 1.2 copy-done.4
  855.5 0.0 copy-start.3
  855.5 0.6 multiply_reduce_fusion.3
  856.0 1.0 copy-done.3
  857.0 0.8 fusion.28
  857.8 77.1 %psum.7 = f32[1024]{0:T(1024)S(1)} all-reduce(f32[1024]{0:T(1024)S(1)} %get-tuple-element.4), channel_id=1, replica_groups=mesh['dp'=32,'fsdp'=8] {'dp','fsdp'}, use_global_device_ids=true, to_apply=%region_7.0 | all-reduce | flops 1024 | bytes 8192 | tf_op jit(solution)/shard_map/psum | solution.py:41
  934.9 2.1 multiply_reduce_fusion.2
  937.1 0.0 copy-start.2
  937.1 2.6 convolution_multiply_fusion
  939.7 0.0 copy-done.2
  939.7 0.3 fusion.6
  940.0 0.1 multiply_reduce_fusion
  940.2 0.1 div.45
  940.3 1.7 fusion.5
  942.0 0.0 copy-start.5
  942.0 6.6 fusion
  948.6 17.6 %copy.9 = bf16[5120,1280]{1,0:T(8,128)(2,1)} copy(bf16[5120,1280]{0,1:T(8,128)(2,1)} %fusion) | data formatting | bytes 26214400
  966.3 0.0 reduce-scatter.7.cloned.1.call-update
  966.3 0.0 reduce-scatter.9.cloned.1.call-start
  966.3 135.0 %reduce-scatter.7.cloned.1.call-done = bf16[640,1280]{1,0:T(8,128)(2,1)} async-done(((bf16[5120,1280]{1,0:T(8,128)(2,1)}), bf16[640,1280]{1,0:T(8,128)(2,1)}) %reduce-scatter.7.cloned.1.call-update) | async-done | bytes 1638416
  1101.4 3.5 copy.10
  1104.9 0.0 reduce-scatter.9.cloned.1.call-update
  1104.9 0.0 copy-done.5
  1104.9 14.5 %convolution_convert_fusion.1 = bf16[256,5120]{1,0:T(8,128)(2,1)} fusion(bf16[256,1280]{1,0:T(8,128)(2,1)S(1)} %fusion.5, bf16[5120,1280]{1,0:T(8,128)(2,1)} %all-gather.4.cloned.1.call-done), kind=kOutput, calls=%fused_computation.2 | convolution fusion | flops 3356753920 | bytes 16384000 | tf_op jit(solution)/shard_map/dot_general | solution.py:66
  1119.4 105.7 %reduce-scatter.9.cloned.1.call-done = bf16[640,40]{0,1:T(8,128)(2,1)} async-done(((bf16[640,1280]{0,1:T(8,128)(2,1)}), bf16[640,40]{0,1:T(8,128)(2,1)}) %reduce-scatter.9.cloned.1.call-update) | async-done | bytes 51216
  1225.1 1.5 convert_element_type.50
  (7 shorter events, 0.0 us)
Async XLA Ops:
  7.2 838.5 %copy-start = (bf16[256,5120]{1,0:T(8,128)(2,1)S(1)}, bf16[256,5120]{1,0:T(8,128)(2,1)}, u32[]{:S(2)}) copy-start(bf16[256,5120]{1,0:T(8,128)(2,1)} %param.6) | copy-start | bytes 7864324
  7.2 698.5 %all-gather.6.cloned.1.call-start = ((), (), s32[]{:S(2)}) async-start(), calls=%async_computation.3 | async-start | bytes 2105344 | tf_op jit(solution)/shard_map/all_gather | solution.py:34
  9.6 836.0 %all-gather.4.cloned.1.call-start = ((), (), s32[]{:S(2)}) async-start(), calls=%async_computation.2 | async-start | bytes 14745600 | tf_op jit(solution)/shard_map/all_gather | solution.py:17
  10.4 1091.0 %reduce-scatter.7.cloned.1.call-start = ((), (), s32[]{:S(2)}) async-start(), calls=%async_computation.4 | async-start | bytes 14745600
  10.4 835.2 %copy-start.7 = (bf16[256,1280]{1,0:T(8,128)(2,1)S(1)}, bf16[256,1280]{1,0:T(8,128)(2,1)}, u32[]{:S(2)}) copy-start(bf16[256,1280]{1,0:T(8,128)(2,1)} %param.7) | copy-start | bytes 1966084
  853.2 1.1 copy-start.1
  853.2 0.7 copy-start.6
  853.2 2.2 copy-start.4
  855.5 1.6 copy-start.3
  937.1 2.6 copy-start.2
  942.0 162.9 %copy-start.5 = (bf16[256,1280]{1,0:T(8,128)(2,1)}, bf16[256,1280]{1,0:T(8,128)(2,1)S(1)}, u32[]{:S(2)}) copy-start(bf16[256,1280]{1,0:T(8,128)(2,1)S(1)} %fusion.5) | copy-start | bytes 1966084
  966.3 258.9 %reduce-scatter.9.cloned.1.call-start = ((), (), s32[]{:S(2)}) async-start(), calls=%async_computation.5 | async-start | bytes 1689600
Sparse Core Ops, SparseCore 0:
  10.5 695.1 all-gather.5
  707.5 138.1 all-gather.3
  966.4 134.9 reduce-scatter.6
  1105.4 119.7 reduce-scatter.8
where the time goes:
time: 1230 us
  waiting for transfers between devices  1070 us (87%)
  blocking collectives  77.1 us (6%)
  matrix products  34.8 us (3%)
  local copies, waits for them, and re-layouts  27.8 us (2%)
  between operations  13.9 us (1%)
    all_gather x1, waiting for transfers between devices, body(): every_opt = lax.all_gather(opt_unit, ('dp', 'fsdp'), axis=0, tiled=True)  695 us
    unnamed x6, waiting for transfers between devices  242 us
    all_gather x1, waiting for transfers between devices, body(): gathered = lax.all_gather(w_down, 'fsdp', axis=0, tiled=True)  136 us
    psum x1, blocking collectives, body(): totals = lax.psum(jnp.sum(powers, axis=0), ('dp', 'fsdp'))  77.1 us
    unnamed x19, local copies, waits for them, and re-layouts  27.7 us
  transfers between devices with their start and end apart: 4, of which 4 were waited for; matrix products, arithmetic and copies ran while one was open for 1% of the time, Pallas kernels for 0%

commit v1 on v0

v1 whole, which is shorter than its diff:
```python
import jax
import jax.numpy as jnp
from jax import lax
from jax.sharding import Mesh, PartitionSpec as P

PATCHES = 64
epsilon = 1e-06
logit_scale = 100.0
bf16 = jnp.bfloat16
f32 = jnp.float32
contract = (((1,), (1,)), ((), ()))
ALL = ("yh", "z", "c", "yl", "x")


def swap_core(v):
    return lax.ppermute(v, "c", [(0, 1), (1, 0)])


def total_sum(v):
    for axes in ("c", "x", ("yh", "yl"), "z"):
        v = lax.psum(v, axes)
    return v


def body(hidden_act, resid, w_down, norm_gain, w_proj, optical):
    tok_rows, ff = hidden_act.shape
    images = tok_rows // PATCHES
    width = resid.shape[1]
    half = width // 2
    shard = w_down.shape[0]
    core = lax.axis_index("c")

    w_part = lax.dynamic_slice_in_dim(w_down, core * half, half, 1)
    w_own = lax.all_gather(w_part, ("yl", "x"), axis=0, tiled=True)
    w_peer = swap_core(w_own)

    opt_full = optical.astype(f32)
    opt_unit = (
        opt_full * lax.rsqrt(jnp.sum(opt_full * opt_full, axis=1, keepdims=True) + epsilon)
    ).astype(bf16)
    every_opt = lax.all_gather(opt_unit, ("yl", "x"), axis=0, tiled=True)
    every_opt = lax.all_gather(every_opt, ("yh", "z", "c"), axis=0, tiled=True)

    hidden_peer = swap_core(hidden_act)

    branch_own = jnp.dot(hidden_act, w_own, preferred_element_type=f32)
    branch_peer = jnp.dot(hidden_act, w_peer, preferred_element_type=f32)
    first = core == 0
    branch = jnp.concatenate(
        [jnp.where(first, branch_own, branch_peer), jnp.where(first, branch_peer, branch_own)], axis=1
    )
    summed = resid.astype(f32) + branch
    center = jnp.mean(summed, axis=1, keepdims=True)
    spread = jnp.mean((summed - center) ** 2, axis=1, keepdims=True)
    inv_std = lax.rsqrt(spread + epsilon)
    normed = (summed - center) * inv_std
    scaled = normed * norm_gain
    pooled = scaled.reshape(images, PATCHES, width).mean(axis=1).astype(bf16)
    embed = jnp.dot(pooled, w_proj, preferred_element_type=f32)
    inv_len = lax.rsqrt(jnp.sum(embed * embed, axis=1, keepdims=True) + epsilon)
    sar_unit = embed * inv_len
    sar_half = sar_unit.astype(bf16)
    scores = logit_scale * lax.dot_general(
        sar_half, every_opt, contract, preferred_element_type=f32
    )
    powers = jnp.exp(scores)
    row_prob = powers / jnp.sum(powers, axis=1, keepdims=True)
    totals = total_sum(jnp.sum(powers, axis=0))
    col_prob = powers / totals[None, :]
    first_pair = lax.axis_index(ALL) * images
    positive = (
        lax.broadcasted_iota(jnp.int32, scores.shape, 1)
        == first_pair + lax.broadcasted_iota(jnp.int32, scores.shape, 0)
    ).astype(f32)
    weights = (row_prob + col_prob - 2.0 * positive).astype(bf16)
    grad_unit = 0.5 * logit_scale * jnp.dot(weights, every_opt, preferred_element_type=f32)
    grad_embed = inv_len * (
        grad_unit - sar_unit * jnp.sum(sar_unit * grad_unit, axis=1, keepdims=True)
    )
    grad_pooled = lax.dot_general(
        grad_embed.astype(bf16), w_proj, contract, preferred_element_type=f32
    )
    grad_tokens = jnp.broadcast_to(
        (grad_pooled / PATCHES)[:, None, :], (images, PATCHES, width)
    ).reshape(tok_rows, width)
    grad_normed = grad_tokens * norm_gain
    grad_sum = inv_std * (
        grad_normed
        - jnp.mean(grad_normed, axis=1, keepdims=True)
        - normed * jnp.mean(grad_normed * normed, axis=1, keepdims=True)
    )
    d_resid = grad_sum.astype(bf16)

    dp_rest = lax.axis_size("yh") * lax.axis_size("z")
    cols = width // (2 * dp_rest)
    place = lax.broadcasted_iota(jnp.int32, (width, width), 1)
    rest = lax.rem(place, half)
    which = lax.rem(place // half + core, 2)
    source = ((rest // cols) * 2 + which) * cols + lax.rem(rest, cols)
    pick = (lax.broadcasted_iota(jnp.int32, (width, width), 0) == source).astype(bf16)
    split = jnp.dot(d_resid, pick, preferred_element_type=f32).astype(bf16)
    d_cat = jnp.concatenate([split[:, :half], swap_core(split[:, half:])], axis=0)
    h_cat = jnp.concatenate([hidden_act, hidden_peer], axis=0)
    d_cat_t = d_cat.T
    terms = jnp.stack(
        [
            jnp.dot(
                d_cat_t, h_cat[:, k * shard : (k + 1) * shard], preferred_element_type=f32
            ).astype(bf16)
            for k in range(ff // shard)
        ]
    )
    group_sum = lax.psum_scatter(terms, ("yl", "x"), scatter_dimension=0, tiled=True)
    d_weight = lax.psum_scatter(
        group_sum.reshape(dp_rest, cols, shard), ("yh", "z"), scatter_dimension=0, tiled=True
    )
    d_weight = d_weight.reshape(cols, shard).astype(f32).T

    d_own = lax.dynamic_slice_in_dim(d_resid, core * half, half, 1)
    d_peer = lax.dynamic_slice_in_dim(d_resid, (1 - core) * half, half, 1)
    d_hidden = (
        lax.dot_general(d_own, w_own, contract, preferred_element_type=f32)
        + lax.dot_general(d_peer, w_peer, contract, preferred_element_type=f32)
    ).astype(bf16)
    return (d_hidden, d_resid, d_weight)


def solution(mesh):
    parts = Mesh(mesh.devices.reshape(2, -1, 2, 2, 4), ALL)
    rows = P(ALL, None)
    in_specs = (rows, rows, P(("yl", "x"), None), P(), P(), rows)
    out_specs = (rows, rows, P(("yl", "x"), ("yh", "z", "c")))
    return jax.shard_map(body, mesh=parts, in_specs=in_specs, out_specs=out_specs, check_vma=False)
```

time: 1230 us -> 491 us (0.40)
  waiting for transfers between devices: 1070 us -> 343 us
  blocking collectives: 77.1 us -> 63.4 us
    all_gather x2, waiting for transfers between devices: 831 us -> 139 us  [the longest x1 78.9 us: body(): w_own = lax.all_gather(w_part, ('yl', 'x'), axis=0, tiled=True)]
    unnamed x6 -> x5, waiting for transfers between devices: 242 us -> 131 us
    reduce_scatter x0 -> x1, waiting for transfers between devices: none -> 72.6 us  [body(): lax.psum_scatter(terms, ('yl', 'x'), scatter_dimension=0, tiled=True)]
    psum x1 -> x4, blocking collectives: 77.1 us -> 35.9 us  [total_sum(): v = lax.psum(v, axes)]
    all_gather x0 -> x1, blocking collectives: none -> 27.6 us  [body(): every_opt = lax.all_gather(opt_unit, ('yl', 'x'), axis=0, tiled=True)]
    unnamed x19 -> x30, local copies, waits for them, and re-layouts: 27.7 us -> 7.67 us
    dot_general x7 -> x17, matrix products: 34.8 us -> 41.9 us  [the longest x8 13 us: body(): jnp.dot(d_cat_t, h_cat[:, k * shard:(k + 1) * shard], preferred_element_t...]
  transfers between devices with their start and end apart: 4 -> 7, of which waited for: 4 -> 4; matrix products, arithmetic and copies ran while one was open for 1% -> 10% of each run, Pallas kernels for 0% -> 0%
where the time goes in v1:
time: 491 us
  waiting for transfers between devices  343 us (70%)
  blocking collectives  63.4 us (13%)
  matrix products  41.9 us (9%)
  local copies, waits for them, and re-layouts  18.7 us (4%)
  between operations  15.8 us (3%)
  other arithmetic  7.71 us (2%)
    unnamed x5, waiting for transfers between devices  131 us
    all_gather x1, waiting for transfers between devices, body(): w_own = lax.all_gather(w_part, ('yl', 'x'), axis=0, tiled=True)  78.9 us
    reduce_scatter x1, waiting for transfers between devices, body(): lax.psum_scatter(terms, ('yl', 'x'), scatter_dimension=0, tiled=True)  72.6 us
    all_gather x1, waiting for transfers between devices, body(): every_opt = lax.all_gather(every_opt, ('yh', 'z', 'c'), axis=0, tiled=True)  59.9 us
    psum x4, blocking collectives, total_sum(): v = lax.psum(v, axes)  35.9 us
    all_gather x1, blocking collectives, body(): every_opt = lax.all_gather(opt_unit, ('yl', 'x'), axis=0, tiled=True)  27.6 us
    dot_general x8, matrix products, body(): jnp.dot(d_cat_t, h_cat[:, k * shard:(k + 1) * shard], preferred_element_t...  13 us
  transfers between devices with their start and end apart: 7, of which 4 were waited for; matrix products, arithmetic and copies ran while one was open for 10% of the time, Pallas kernels for 0%

profile of v1, /device:TPU:2, one launch (start us, length us, event | category | flops | bytes accessed | tf_op | source)
XLA Modules:
  0.0 490.6 jit_solution(1856416377885000776)
XLA Ops:
  8.0 0.0 copy-start
  8.0 0.0 all-gather.4.cloned.1.call-start
  8.1 2.3 constant_dynamic-slice_fusion
  10.3 0.0 all-gather.4.cloned.1.call-update
  10.4 0.0 all-gather.6.cloned.1.call-start
  10.4 78.9 %all-gather.4.cloned.1.call-done = bf16[5120,640]{1,0:T(8,128)(2,1)} async-done(((bf16[640,640]{1,0:T(8,128)(2,1)}), bf16[5120,640]{1,0:T(8,128)(2,1)}) %all-gather.4.cloned.1.call-update) | async-done | bytes 6553616 | tf_op jit(solution)/shard_map/all_gather | solution.py:34
  89.3 0.1 fusion.53
  89.4 0.1 fusion.60
  89.5 27.6 %all-gather = bf16[8,4,1024]{2,1,0:T(4,128)(2,1)S(1)} all-gather(bf16[1,4,1024]{2,1,0:T(4,128)(2,1)S(1)} %fusion.60), channel_id=1, replica_groups=mesh['yh'=2,'z'=8,'c'=2,'yl'=2,'x'=4] {'yl','x'}, dimensions={0}, use_global_device_ids=true | all-gather | bytes 73728 | tf_op jit(solution)/shard_map/all_gather | solution.py:41
  117.1 0.6 reshape.70
  117.7 0.0 all-gather.6.cloned.1.call-update
  117.7 0.0 reduce-scatter.5.cloned.1.call-start
  117.8 0.1 collective-permute-start.2
  117.9 1.3 copy.16
  119.3 3.5 constant_dynamic-update-slice_fusion.1
  122.9 4.8 fusion.86
  127.7 4.8 select_bitcast_fusion.1
  132.4 0.0 copy-start.3
  132.5 0.2 fusion.83
  132.7 0.3 multiply_reduce_fusion.2
  133.0 0.3 copy-done.1
  133.3 0.2 copy-done.3
  133.5 1.3 fusion.40
  134.8 2.8 copy.17
  137.6 1.4 bitcast_reduce_fusion
  139.0 0.6 multiply_reduce_fusion.4
  139.6 59.9 %all-gather.6.cloned.1.call-done = bf16[1024,1024]{1,0:T(8,128)(2,1)} async-done(((bf16[32,1024]{1,0:T(8,128)(2,1)}), bf16[1024,1024]{1,0:T(8,128)(2,1)}) %all-gather.6.cloned.1.call-update) | async-done | bytes 2097168 | tf_op jit(solution)/shard_map/all_gather | solution.py:42
  199.5 2.4 fusion.84
  201.8 2.5 psum.28
  204.3 8.6 %psum.29 = f32[1024]{0:T(1024)S(1)} all-reduce(f32[1024]{0:T(1024)S(1)} %psum.28), channel_id=1, replica_groups=mesh['yh'=2,'z'=8,'c'=2,'yl'=2,'x'=4] {'x'}, use_global_device_ids=true, to_apply=%region_8.9 | all-reduce | flops 1024 | bytes 8192 | tf_op jit(solution)/shard_map/psum | solution.py:21
  212.9 8.9 %psum.30 = f32[1024]{0:T(1024)S(1)} all-reduce(f32[1024]{0:T(1024)S(1)} %psum.29), channel_id=1, replica_groups=mesh['yh'=2,'z'=8,'c'=2,'yl'=2,'x'=4] {'yh','yl'}, use_global_device_ids=true, to_apply=%region_9.10 | all-reduce | flops 1024 | bytes 8192 | tf_op jit(solution)/shard_map/psum | solution.py:21
  221.7 15.9 %psum.31 = f32[1024]{0:T(1024)S(1)} all-reduce(f32[1024]{0:T(1024)S(1)} %psum.30), channel_id=1, replica_groups=mesh['yh'=2,'z'=8,'c'=2,'yl'=2,'x'=4] {'z'}, use_global_device_ids=true, to_apply=%region_10.11 | all-reduce | flops 1024 | bytes 8192 | tf_op jit(solution)/shard_map/psum | solution.py:21
  237.7 2.1 multiply_reduce_fusion.3
  239.8 0.8 convolution_multiply_fusion
  240.6 1.2 broadcast_in_dim.2
  241.8 2.8 copy.18
  244.6 0.1 multiply_reduce_fusion.1
  244.7 0.1 div.57
  244.8 2.2 multiply_reduce_fusion
  247.0 0.3 copy-done.5
  247.3 0.4 multiply_convert_fusion
  247.7 0.0 copy-start.6
  247.8 1.7 fusion.20
  249.5 0.1 fusion.85
  249.5 0.3 collective-permute-start.1
  249.8 0.2 slice-done.1
  250.1 1.9 constant_dynamic-update-slice_fusion
  252.0 1.6 fusion.24
  253.6 1.6 fusion.26
  255.2 1.6 fusion.28
  256.9 1.6 fusion.30
  258.5 1.6 fusion.32
  260.1 1.6 fusion.34
  261.7 1.7 fusion.36
  263.3 1.6 fusion.38
  264.9 0.0 reduce-scatter.5.cloned.1.call-update
  265.0 0.0 reduce-scatter.7.cloned.1.call-start
  265.0 72.6 %reduce-scatter.5.cloned.1.call-done = bf16[1,640,640]{2,1,0:T(8,128)(2,1)} async-done(((bf16[8,640,640]{2,1,0:T(8,128)(2,1)}), bf16[1,640,640]{2,1,0:T(8,128)(2,1)}) %reduce-scatter.5.cloned.1.call-update) | async-done | bytes 819216 | tf_op jit(solution)/shard_map/reduce_scatter | solution.py:113
  337.6 0.0 reduce-scatter.7.cloned.1.call-update
  337.7 1.1 copy.19
  338.8 5.1 %fusion.50 = f32[256,5120]{1,0:T(8,128)S(1)} fusion(bf16[5120,640]{1,0:T(8,128)(2,1)} %all-gather.4.cloned.1.call-done, bf16[256,1280]{0,1:T(8,128)(2,1)S(1)} %copy-done.7, s32[]{:T(128)S(6)} %select_n.34), kind=kOutput, calls=%fused_computation.71 | convolution fusion | flops 1677721600 | bytes 12124164 | tf_op jit(solution)/shard_map/dot_general | solution.py:122
  343.9 6.7 %fusion.7 = bf16[256,5120]{1,0:T(8,128)(2,1)} fusion(f32[256,5120]{1,0:T(8,128)S(1)} %fusion.50, bf16[5120,640]{1,0:T(8,128)(2,1)} %collective-permute-done, bf16[256,1280]{0,1:T(8,128)(2,1)S(1)} %copy-done.7, s32[]{:T(128)S(6)} %select_n.39), kind=kOutput, calls=%fused_computation.9 | convolution fusion | flops 1680343040 | bytes 14745604 | tf_op jit(solution)/shard_map/dot_general | solution.py:123
  350.6 131.1 %reduce-scatter.7.cloned.1.call-done = bf16[1,40,640]{2,1,0:T(8,128)(2,1)} async-done(((bf16[16,40,640]{2,1,0:T(8,128)(2,1)}), bf16[1,40,640]{2,1,0:T(8,128)(2,1)}) %reduce-scatter.7.cloned.1.call-update) | async-done | bytes 51216
  481.7 1.5 convert_bitcast_fusion
  (35 shorter events, 0.2 us)
Async XLA Ops:
  8.0 131.0 %copy-start = (bf16[1280,1024]{1,0:T(8,128)(2,1)S(1)}, bf16[1280,1024]{1,0:T(8,128)(2,1)}, u32[]{:S(2)}) copy-start(bf16[1280,1024]{1,0:T(8,128)(2,1)} %param.10) | copy-start | bytes 7864324
  8.0 81.3 %copy-start.10 = (bf16[4,1024]{1,0:T(4,128)(2,1)S(1)}, bf16[4,1024]{1,0:T(4,128)(2,1)}, u32[]{:S(2)}) copy-start(bf16[4,1024]{1,0:T(4,128)(2,1)} %param.11) | copy-start | bytes 24580
  8.0 81.2 %all-gather.4.cloned.1.call-start = ((), (), s32[]{:S(2)}) async-start(), calls=%async_computation.2 | async-start | bytes 7372800 | tf_op jit(solution)/shard_map/all_gather | solution.py:34
  10.4 189.1 %all-gather.6.cloned.1.call-start = ((), (), s32[]{:S(2)}) async-start(), calls=%async_computation.3 | async-start | bytes 2162688 | tf_op jit(solution)/shard_map/all_gather | solution.py:42
  89.3 38.4 %collective-permute-start = (bf16[5120,640]{1,0:T(8,128)(2,1)}, bf16[5120,640]{1,0:T(8,128)(2,1)}, u32[]{:S(2)}, u32[]{:S(2)}) collective-permute-start(bf16[5120,640]{1,0:T(8,128)(2,1)} %all-gather.4.cloned.1.call-done), channel_id=1, source_target_pairs={{0,8},{8,0},{1,9},{9,1},{2,10},{10,2},{3,11},{11,3},{4,12},{12,4},... | collective-permute-start | bytes 19660808 | tf_op jit(solution)/shard_map/ppermute | solution.py:16
  117.7 219.9 %reduce-scatter.5.cloned.1.call-start = ((), (), s32[]{:S(2)}) async-start(), calls=%async_computation.4 | async-start | bytes 7372800 | tf_op jit(solution)/shard_map/reduce_scatter | solution.py:113
  117.8 132.0 %collective-permute-start.2 = (bf16[256,5120]{1,0:T(8,128)(2,1)}, bf16[256,5120]{1,0:T(8,128)(2,1)}, u32[]{:S(2)}, u32[]{:S(2)}) collective-permute-start(bf16[256,5120]{1,0:T(8,128)(2,1)} %param.6), channel_id=1, source_target_pairs={{0,8},{8,0},{1,9},{9,1},{2,10},{10,2},{3,11},{11,3},{4,12},{12,4},... | collective-permute-start | bytes 7864328 | tf_op jit(solution)/shard_map/ppermute | solution.py:16
  119.3 3.5 copy-start.8
  132.4 0.8 copy-start.1
  132.4 1.0 copy-start.3
  132.4 1.0 copy-start.9
  244.8 2.2 copy-start.2
  244.8 2.2 copy-start.4
  244.8 2.5 copy-start.5
  247.3 2.6 slice-start
  247.7 1.7 copy-start.6
  247.8 2.3 slice-start.1
  249.5 2.4 collective-permute-start.1
  264.9 72.7 %copy-start.7 = (bf16[256,1280]{0,1:T(8,128)(2,1)S(1)}, bf16[256,1280]{0,1:T(8,128)(2,1)}, u32[]{:S(2)}) copy-start(bf16[256,1280]{0,1:T(8,128)(2,1)} %copy-done.6) | copy-start | bytes 1966084
  265.0 216.8 %reduce-scatter.7.cloned.1.call-start = ((), (), s32[]{:S(2)}) async-start(), calls=%async_computation.5 | async-start | bytes 870400
Sparse Core Ops, SparseCore 0:
  11.2 77.9 all-gather.3
  265.1 72.4 reduce-scatter.4
Sparse Core Ops, SparseCore 1:
  117.8 81.6 all-gather.5
  337.7 143.9 reduce-scatter.6
